TPU v7x, 512 devices: a whole 4x8x8 slice. The times are simulated.
512 devices in a mesh: cfg: 2 (over core), clip: 8 (over x, z_hi), sp: 32 (over z_lo, y).
Axes of the slice: x: 4, y: 8, z: 8 (z_hi: 2, z_lo: 4; z = z_hi * 4 + z_lo), core: 2. Of those that a mesh axis runs over, the one named last changes fastest.
Arguments:
- self_queries: bfloat16 [8, 2, 2560, 4096], P('clip', 'cfg', 'sp'), may hold values from -256 to 256
- self_keys: bfloat16 [8, 2, 2560, 4096], P('clip', 'cfg', 'sp'), may hold values from -8 to 8
- self_values: bfloat16 [8, 2, 2560, 4096], P('clip', 'cfg', 'sp'), may hold values from -6 to 6
- cross_queries: bfloat16 [8, 2, 2560, 4096], P('clip', 'cfg', 'sp'), may hold values from -256 to 256
- text_keys: bfloat16 [2, 512, 4096], P('cfg', 'clip', 'sp'), may hold values from -8 to 8
- text_values: bfloat16 [2, 512, 4096], P('cfg', 'clip', 'sp'), may hold values from -6 to 6
- text_lengths: int32 [2], P('cfg'), may hold values from 64 to 512, as said below
- head_weight: bfloat16 [4096, 64], replicated, may hold values from -0.09375 to 0.09375
- latent: float32 [8, 2560, 64], P('clip', 'sp', 'cfg'), may hold values from -6 to 6
- previous_denoised: float32 [8, 2560, 64], P('clip', 'sp', 'cfg'), may hold values from -6 to 6
- step_index: int32 [8], P('clip'), may hold values from 2 to 48
Outputs:
- denoised: float32 [8, 2560, 64], P('clip', 'sp', 'cfg')
- next_latent: float32 [8, 2560, 64], P('clip', 'sp', 'cfg')
Inputs may be any that keep to these rules, and one draw needn't show every extreme that they name: `text_lengths`: one of the two branches uses all 512 prompt tokens.
All inputs are finite; a program needn't handle non-finite values.
Results may differ from a plain program's by a relative error of at most 0.0009.
The roundings to bfloat16 on the way count: a program that leaves them out, or rounds other values in their place, can miss the bound.
Values may be sent and summed in bfloat16 or wider, within the bound.
A program may use at most 64 MiB of HBM per device.

v0:
```python
import math

import jax
import jax.numpy as jnp
from jax import lax
from jax.sharding import PartitionSpec as P

HEAD_SIZE = 128
STEPS = 50


guide_scale = 5.0
shift_factor = 5.0


def from_partner(value, axis, stride):
    mask = 2**stride
    pairs = [(source, source ^ mask) for source in range(lax.axis_size(axis))]
    return lax.ppermute(value, axis, pairs)


def softmax_rows(scores):
    row_max = jnp.max(scores, axis=-1, keepdims=True)
    shifted = jnp.exp(scores - row_max)
    return (shifted / jnp.sum(shifted, axis=-1, keepdims=True)).astype(jnp.bfloat16)


def attend(queries, key_rows, value_rows, text_limit):
    row_count = queries.shape[0]
    head_count = queries.shape[1] // HEAD_SIZE
    key_count = key_rows.shape[0]
    key_heads = key_rows.reshape(key_count, head_count, HEAD_SIZE)
    value_heads = value_rows.reshape(key_count, head_count, HEAD_SIZE)
    block_rows = 512
    grouped = queries.reshape(row_count // block_rows, block_rows, head_count, HEAD_SIZE)

    def one_block(query_block):
        scores = jnp.einsum(
            "qhd,khd->hqk", query_block, key_heads, preferred_element_type=jnp.float32
        ) * (1.0 / math.sqrt(HEAD_SIZE))
        if text_limit is not None:
            scores = jnp.where(
                jnp.arange(key_count, dtype=jnp.int32)[None, None, :] < text_limit, scores, -1e30
            )
        weights = softmax_rows(scores)
        return jnp.einsum("hqk,khd->qhd", weights, value_heads, preferred_element_type=jnp.float32)

    return lax.map(one_block, grouped).reshape(row_count, head_count * HEAD_SIZE)


def sigma_at(position):
    level = 1.0 - position / STEPS
    return shift_factor * level / (1.0 + (shift_factor - 1.0) * level)


def log_ratio(sigma_value):
    return jnp.log(1.0 - sigma_value) - jnp.log(sigma_value)


def project_rows(rows, weight_rows):
    return jnp.dot(
        rows,
        weight_rows.astype(jnp.float32),
        precision=lax.Precision.HIGHEST,
        preferred_element_type=jnp.float32,
    )


def on_device(
    self_queries,
    self_keys,
    self_values,
    cross_queries,
    text_keys,
    text_values,
    text_lengths,
    head_weight,
    latent,
    previous_denoised,
    step_index,
):
    tok_rows = self_queries.shape[2]
    width = self_queries.shape[3]
    lat_half = latent.shape[2]
    branch = lax.axis_index("cfg")
    flat = lambda array: array.reshape(tok_rows, width)
    prompt_keys, prompt_values = (
        lax.all_gather(text_keys, "clip", axis=1, tiled=True),
        lax.all_gather(text_values, "clip", axis=1, tiled=True),
    )
    prompt_keys = prompt_keys[0]
    prompt_values = prompt_values[0]
    text_limit = text_lengths[0]
    query_rows, key_rows, value_rows, cross_rows = (
        lax.all_to_all(flat(self_queries), "sp", split_axis=1, concat_axis=0, tiled=True),
        lax.all_to_all(flat(self_keys), "sp", split_axis=1, concat_axis=0, tiled=True),
        lax.all_to_all(flat(self_values), "sp", split_axis=1, concat_axis=0, tiled=True),
        lax.all_to_all(flat(cross_queries), "sp", split_axis=1, concat_axis=0, tiled=True),
    )
    self_out = attend(query_rows, key_rows, value_rows, None)
    cross_out = attend(cross_rows, prompt_keys, prompt_values, text_limit)
    attended = (self_out + cross_out).astype(jnp.bfloat16)
    returned = lax.all_to_all(attended, "sp", split_axis=0, concat_axis=1, tiled=True)
    partner = from_partner(returned, "cfg", 0)
    conditional = jnp.where(branch == 0, returned, partner).astype(jnp.float32)
    unconditional = jnp.where(branch == 0, partner, returned).astype(jnp.float32)
    guided = unconditional + guide_scale * (conditional - unconditional)
    own_columns = lax.dynamic_slice_in_dim(head_weight, branch * lat_half, lat_half, 1)
    velocity = project_rows(guided, own_columns)
    position = step_index[0].astype(jnp.float32)
    sigma_now = sigma_at(position)
    sigma_next = sigma_at(position + 1.0)
    sigma_prev = sigma_at(position - 1.0)
    denoised = latent - sigma_now * velocity[None]
    lambda_now = log_ratio(sigma_now)
    h_value = log_ratio(sigma_next) - lambda_now
    phi_value = jnp.expm1(-h_value)
    ratio = (log_ratio(sigma_prev) - lambda_now) / h_value
    difference = (denoised - previous_denoised) / ratio
    next_latent = (
        sigma_next / sigma_now * latent
        - (1.0 - sigma_next) * phi_value * denoised
        - 0.5 * (1.0 - sigma_next) * phi_value * difference
    )
    return (denoised, next_latent)


def solution(mesh):
    return jax.shard_map(
        on_device,
        mesh=mesh,
        in_specs=(
            P("clip", "cfg", "sp", None),
            P("clip", "cfg", "sp", None),
            P("clip", "cfg", "sp", None),
            P("clip", "cfg", "sp", None),
            P("cfg", "clip", "sp"),
            P("cfg", "clip", "sp"),
            P("cfg"),
            P(),
            P("clip", "sp", "cfg"),
            P("clip", "sp", "cfg"),
            P("clip"),
        ),
        out_specs=(P("clip", "sp", "cfg"), P("clip", "sp", "cfg")),
        check_vma=False,
    )
```

profile of v0, /device:TPU:1, one launch (start us, length us, event | category | flops | bytes accessed | tf_op | source)
XLA Modules:
  0.0 245.0 jit_solution(10951478449828738296)
XLA Ops:
  0.6 1.3 copy.35
  3.0 13.5 %all-to-all-start = ((bf16[80,32,128]{2,0,1:T(8,128)(2,1)}), bf16[80,32,128]{2,0,1:T(8,128)(2,1)S(1)}, u32[]{:S(2)}, u32[]{:S(2)}) async-start(bf16[80,32,128]{2,0,1:T(8,128)(2,1)} %copy.27), calls=%async_computation | async-start | bytes 1310720 | tf_op jit(solution)/shard_map/all_to_all | solution.py:95
  16.7 1.1 copy.28
  17.8 16.0 %all-to-all-done = bf16[80,32,128]{2,0,1:T(8,128)(2,1)S(1)} async-done(((bf16[80,32,128]{2,0,1:T(8,128)(2,1)}), bf16[80,32,128]{2,0,1:T(8,128)(2,1)S(1)}, u32[]{:S(2)}, u32[]{:S(2)}) %all-to-all-start) | async-done | bytes 655392 | tf_op jit(solution)/shard_map/all_to_all | solution.py:95
  33.8 7.9 %all-to-all-start.1 = ((bf16[80,32,128]{2,0,1:T(8,128)(2,1)}), bf16[80,32,128]{2,0,1:T(8,128)(2,1)S(1)}, u32[]{:S(2)}, u32[]{:S(2)}) async-start(bf16[80,32,128]{2,0,1:T(8,128)(2,1)} %copy.28), calls=%async_computation.1 | async-start | bytes 1310720 | tf_op jit(solution)/shard_map/all_to_all | solution.py:96
  41.8 1.1 copy.29
  42.9 16.1 %all-to-all-done.1 = bf16[80,32,128]{2,0,1:T(8,128)(2,1)S(1)} async-done(((bf16[80,32,128]{2,0,1:T(8,128)(2,1)}), bf16[80,32,128]{2,0,1:T(8,128)(2,1)S(1)}, u32[]{:S(2)}, u32[]{:S(2)}) %all-to-all-start.1) | async-done | bytes 655392 | tf_op jit(solution)/shard_map/all_to_all | solution.py:96
  59.0 7.7 %all-to-all-start.2 = ((bf16[80,32,128]{2,0,1:T(8,128)(2,1)}), bf16[80,32,128]{2,0,1:T(8,128)(2,1)S(1)}, u32[]{:S(2)}, u32[]{:S(2)}) async-start(bf16[80,32,128]{2,0,1:T(8,128)(2,1)} %copy.29), calls=%async_computation.2 | async-start | bytes 1310720 | tf_op jit(solution)/shard_map/all_to_all | solution.py:97
  66.9 1.1 copy.31
  68.0 42.5 %all_gather.6 = bf16[1,512,128]{2,1,0:T(8,128)(2,1)S(1)} all-gather(bf16[1,64,128]{2,1,0:T(8,128)(2,1)S(1)} %copy-done.8), channel_id=1, replica_groups=mesh['cfg'=2,'clip'=8,'sp'=32] {'clip'}, dimensions={1}, use_global_device_ids=true | all-gather | bytes 147456 | tf_op jit(solution)/shard_map/all_gather | solution.py:88
  110.5 37.6 %all_gather.7 = bf16[1,512,128]{2,1,0:T(8,128)(2,1)S(1)} all-gather(bf16[1,64,128]{2,1,0:T(8,128)(2,1)S(1)} %copy-done.9), channel_id=1, replica_groups=mesh['cfg'=2,'clip'=8,'sp'=32] {'clip'}, dimensions={1}, use_global_device_ids=true | all-gather | bytes 147456 | tf_op jit(solution)/shard_map/all_gather | solution.py:89
  149.0 17.4 %all-to-all-start.3 = ((bf16[80,32,128]{2,0,1:T(8,128)(2,1)}), bf16[80,32,128]{2,0,1:T(8,128)(2,1)S(1)}, u32[]{:S(2)}, u32[]{:S(2)}) async-start(bf16[80,32,128]{2,0,1:T(8,128)(2,1)} %copy.31), calls=%async_computation.3 | async-start | bytes 1310720 | tf_op jit(solution)/shard_map/all_to_all | solution.py:98
  166.5 21.9 %while.20 = (s32[]{:T(128)}, f32[5,512,1,128]{3,1,2,0:T(8,128)S(1)}, bf16[5,512,1,128]{3,1,2,0:T(8,128)(2,1)}, bf16[2560,1,128]{2,0,1:T(8,128)(2,1)S(1)}, bf16[2560,1,128]{2,0,1:T(8,128)(2,1)}, /*index=5*/s32[]{:T(128)}) while((s32[]{:T(128)}, f32[5,512,1,128]{3,1,2,0:T(8,128)S(1)}, bf16[5,512,1,128]{3,1,2,0:T(8,128)(2,1)}, ...), condition=%wide.region_3.4_spmd, body=%wide.region_0.3_spmd.sunk | while | flops 680262656 | bytes 20064868 | solution.py:48
  166.5 1.8 fusion.45
  169.4 1.4 fusion.47
  170.9 1.8 fusion.45
  173.8 1.4 fusion.47
  175.3 1.8 fusion.45
  178.2 1.4 fusion.47
  179.6 1.8 fusion.45
  182.6 1.4 fusion.47
  184.0 1.8 fusion.45
  186.9 1.4 fusion.47
  189.3 12.4 %while.21 = (s32[]{:T(128)}, f32[5,512,1,128]{3,1,2,0:T(8,128)S(1)}, s32[]{:T(128)}, bf16[5,512,1,128]{3,1,2,0:T(8,128)(2,1)}, bf16[512,1,128]{2,0,1:T(8,128)(2,...) while((s32[]{:T(128)}, f32[5,512,1,128]{3,1,2,0:T(8,128)S(1)}, s32[]{:T(128)}, ...), condition=%wide.region_7.8_spmd, body=%wide.region_4.7_spmd.sunk | while | flops 136314368 | bytes 3812949 | solution.py:48
  190.0 1.2 fusion.49
  192.5 1.2 fusion.49
  195.0 1.2 fusion.49
  197.5 1.2 fusion.49
  199.9 1.2 fusion.49
  201.9 23.2 %all_to_all.80 = bf16[32,80,128]{2,1,0:T(8,128)(2,1)S(1)} all-to-all(bf16[32,80,128]{2,1,0:T(8,128)(2,1)S(1)} %bitcast.129), channel_id=1, replica_groups=mesh['cfg'=2,'clip'=8,'sp'=32] {'sp'}, dimensions={0} | all-to-all | bytes 1310720 | tf_op jit(solution)/shard_map/all_to_all | solution.py:103
  225.2 16.4 %collective-permute-start = (bf16[80,4096]{1,0:T(8,128)(2,1)S(1)}, bf16[80,4096]{1,0:T(8,128)(2,1)S(1)}, u32[]{:S(2)}, u32[]{:S(2)}) collective-permute-start(bf16[80,4096]{1,0:T(8,128)(2,1)S(1)} %copy_bitcast_fusion), channel_id=1, source_target_pairs={{0,256},{256,0},{1,257},{257,1},{2,258},{258,2},{3,259},{259,3},{4... | collective-permute-start | bytes 1966088 | tf_op jit(solution)/shard_map/ppermute | solution.py:19
  243.4 1.6 multiply_subtract_fusion
  (63 shorter events, 15.7 us)
Async XLA Ops:
  0.6 242.7 %copy-start = (bf16[4096,64]{0,1:T(8,128)(2,1)S(1)}, bf16[4096,64]{0,1:T(8,128)(2,1)}, u32[]{:S(2)}) copy-start(bf16[4096,64]{0,1:T(8,128)(2,1)} %param.22) | copy-start | bytes 1572868
  1.9 14.6 %copy-start.3 = (bf16[1,1,80,4096]{3,2,1,0:T(8,128)(2,1)S(1)}, bf16[1,1,80,4096]{3,2,1,0:T(8,128)(2,1)}, u32[]{:S(2)}) copy-start(bf16[1,1,80,4096]{3,2,1,0:T(8,128)(2,1)} %param.16) | copy-start | bytes 1966084
  3.0 30.7 %all-to-all-start = ((bf16[80,32,128]{2,0,1:T(8,128)(2,1)}), bf16[80,32,128]{2,0,1:T(8,128)(2,1)S(1)}, u32[]{:S(2)}, u32[]{:S(2)}) async-start(bf16[80,32,128]{2,0,1:T(8,128)(2,1)} %copy.27), calls=%async_computation | async-start | bytes 1310720 | tf_op jit(solution)/shard_map/all_to_all | solution.py:95
  16.6 25.0 %copy-start.4 = (bf16[1,1,80,4096]{3,2,1,0:T(8,128)(2,1)S(1)}, bf16[1,1,80,4096]{3,2,1,0:T(8,128)(2,1)}, u32[]{:S(2)}) copy-start(bf16[1,1,80,4096]{3,2,1,0:T(8,128)(2,1)} %param.17) | copy-start | bytes 1966084
  33.8 8.0 %copy-start.2 = (bf16[80,32,128]{2,0,1:T(8,128)(2,1)}, bf16[80,32,128]{2,0,1:T(8,128)(2,1)S(1)}, u32[]{:S(2)}) copy-start(bf16[80,32,128]{2,0,1:T(8,128)(2,1)S(1)} %all-to-all-done) | copy-start | bytes 1966084
  33.8 25.3 %all-to-all-start.1 = ((bf16[80,32,128]{2,0,1:T(8,128)(2,1)}), bf16[80,32,128]{2,0,1:T(8,128)(2,1)S(1)}, u32[]{:S(2)}, u32[]{:S(2)}) async-start(bf16[80,32,128]{2,0,1:T(8,128)(2,1)} %copy.28), calls=%async_computation.1 | async-start | bytes 1310720 | tf_op jit(solution)/shard_map/all_to_all | solution.py:96
  41.8 25.0 %copy-start.5 = (bf16[1,1,80,4096]{3,2,1,0:T(8,128)(2,1)S(1)}, bf16[1,1,80,4096]{3,2,1,0:T(8,128)(2,1)}, u32[]{:S(2)}) copy-start(bf16[1,1,80,4096]{3,2,1,0:T(8,128)(2,1)} %param.18) | copy-start | bytes 1966084
  59.0 89.1 %all-to-all-start.2 = ((bf16[80,32,128]{2,0,1:T(8,128)(2,1)}), bf16[80,32,128]{2,0,1:T(8,128)(2,1)S(1)}, u32[]{:S(2)}, u32[]{:S(2)}) async-start(bf16[80,32,128]{2,0,1:T(8,128)(2,1)} %copy.29), calls=%async_computation.2 | async-start | bytes 1310720 | tf_op jit(solution)/shard_map/all_to_all | solution.py:97
  66.7 1.3 copy-start.8
  66.8 43.7 %copy-start.9 = (bf16[1,64,128]{2,1,0:T(8,128)(2,1)S(1)}, bf16[1,64,128]{2,1,0:T(8,128)(2,1)}, u32[]{:S(2)}) copy-start(bf16[1,64,128]{2,1,0:T(8,128)(2,1)} %param.20) | copy-start | bytes 49156
  148.1 0.9 copy-start.6
  149.0 39.4 %all-to-all-start.3 = ((bf16[80,32,128]{2,0,1:T(8,128)(2,1)}), bf16[80,32,128]{2,0,1:T(8,128)(2,1)S(1)}, u32[]{:S(2)}, u32[]{:S(2)}) async-start(bf16[80,32,128]{2,0,1:T(8,128)(2,1)} %copy.31), calls=%async_computation.3 | async-start | bytes 1310720 | tf_op jit(solution)/shard_map/all_to_all | solution.py:98
  168.3 1.1 copy-start.7
  172.7 1.1 copy-start.7
  177.1 1.1 copy-start.7
  181.5 1.1 copy-start.7
  185.9 1.1 copy-start.7
  188.4 0.8 copy-start.1
  201.9 41.4 %copy-start.10 = (f32[1,80,32]{1,2,0:T(8,128)S(1)}, f32[1,80,32]{1,2,0:T(8,128)}, u32[]{:S(2)}) copy-start(f32[1,80,32]{1,2,0:T(8,128)} %param.24) | copy-start | bytes 30724
  201.9 41.4 %copy-start.11 = (f32[1,80,32]{1,2,0:T(8,128)S(1)}, f32[1,80,32]{1,2,0:T(8,128)}, u32[]{:S(2)}) copy-start(f32[1,80,32]{1,2,0:T(8,128)} %param.23) | copy-start | bytes 30724
  225.2 18.1 %collective-permute-start = (bf16[80,4096]{1,0:T(8,128)(2,1)S(1)}, bf16[80,4096]{1,0:T(8,128)(2,1)S(1)}, u32[]{:S(2)}, u32[]{:S(2)}) collective-permute-start(bf16[80,4096]{1,0:T(8,128)(2,1)S(1)} %copy_bitcast_fusion), channel_id=1, source_target_pairs={{0,256},{256,0},{1,257},{257,1},{2,258},{258,2},{3,259},{259,3},{4... | collective-permute-start | bytes 1966088 | tf_op jit(solution)/shard_map/ppermute | solution.py:19
where the time goes:
time: 246 us; the launch traced here: 245 us
  blocking collectives  103 us (42%)
  starting transfers between devices  62.8 us (26%)
  waiting for transfers between devices  32.7 us (13%)
  matrix products  25.9 us (11%)
  local copies, waits for them, and re-layouts  9.27 us (4%)
  other arithmetic  8.57 us (3%)
    all_gather x1, blocking collectives, on_device(): lax.all_gather(text_keys, 'clip', axis=1, tiled=True)  42.5 us
    all_gather x1, blocking collectives, on_device(): lax.all_gather(text_values, 'clip', axis=1, tiled=True)  37.6 us
    all_to_all x1, blocking collectives, on_device(): lax.all_to_all(attended, 'sp', split_axis=0, concat_axis=1, tiled=True)  23.2 us
    all_to_all x1, starting transfers between devices, on_device(): lax.all_to_all(flat(cross_queries), 'sp', split_axis=1, concat_axis=0, ti...  17.4 us
    ppermute x1, starting transfers between devices, from_partner(): return lax.ppermute(value, axis, pairs)  16.4 us
    all_to_all x1, waiting for transfers between devices, on_device(): lax.all_to_all(flat(self_keys), 'sp', split_axis=1, concat_axis=0, tiled=...  16.1 us
    all_to_all x1, waiting for transfers between devices, on_device(): lax.all_to_all(flat(self_queries), 'sp', split_axis=1, concat_axis=0, til...  16 us
    dot_general x10, matrix products, one_block(): jnp.einsum('qhd,khd->hqk', query_block, key_heads, preferred_element_type...  15.3 us
  transfers between devices with their start and end apart: 5, of which 3 were waited for; matrix products, arithmetic and copies ran while one was open for 10% of the time, Pallas kernels for 0%

commit v1 on v0

v1 whole, which is shorter than its diff:
```python
import math

import jax
import jax.numpy as jnp
from jax import lax
from jax.experimental import pallas as pl
from jax.experimental.pallas import tpu as pltpu
from jax.sharding import PartitionSpec as P

HEAD_SIZE = 128
STEPS = 50
MESH = pl.DeviceIdType.MESH

guide_scale = 5.0
shift_factor = 5.0

Y = 8
Z = 4
PEERS = Y * Z
TOKENS = 80
PAIRS = PEERS // 2
PACK = 24
SCORE_SCALE = math.log2(math.e) / math.sqrt(HEAD_SIZE)
NT = (((1,), (1,)), ((), ()))
TN = (((0,), (0,)), ((), ()))


def sigma_at(position):
    level = 1.0 - position / STEPS
    return shift_factor * level / (1.0 + (shift_factor - 1.0) * level)


def log_ratio(sigma_value):
    return jnp.log(1.0 - sigma_value) - jnp.log(sigma_value)


def attend(queries, keys, values, text_limit):
    scores = lax.dot_general(queries, keys, NT, preferred_element_type=jnp.float32)
    if text_limit is not None:
        positions = lax.broadcasted_iota(jnp.int32, scores.shape, 1)
        scores = jnp.where(positions < text_limit, scores, -1e30)
    row_max = jnp.max(scores, axis=-1, keepdims=True)
    shifted = jnp.exp2((scores - row_max) * SCORE_SCALE)
    inverse = 1.0 / jnp.sum(shifted, axis=-1, keepdims=True)
    weights = (shifted * inverse).astype(jnp.bfloat16)
    return jnp.dot(weights, values, preferred_element_type=jnp.float32)


def offsets(slot):
    step = lax.rem(PEERS - slot, PEERS)
    ring, dz = lax.div(step, Z), lax.rem(step, Z)
    dy = lax.div(ring + 1, 2) * (2 * lax.rem(ring, 2) - 1)
    return dy, dz


def kernel(
    limit_ref,
    step_ref,
    q_ref,
    k_ref,
    v_ref,
    c_ref,
    tk_ref,
    tv_ref,
    w_ref,
    latent_ref,
    previous_ref,
    denoised_ref,
    next_ref,
    q_buf,
    k_buf,
    v_buf,
    c_buf,
    tk_buf,
    tv_buf,
    w_buf,
    spread,
    mine,
    part_out,
    part_in,
    back_out,
    back_in,
    send_sem,
    recv_sem,
    text_send,
    text_recv,
    local_sem,
    part_send,
    part_recv,
    back_send,
    back_recv,
):
    core = lax.axis_index("cfg")
    clip = lax.axis_index("clip")
    sp = lax.axis_index("sp")
    my_y, my_z = lax.rem(sp, Y), lax.div(sp, Y)
    my_x, my_far = lax.div(clip, 2), lax.rem(clip, 2)
    far_clip = my_x * 2 + (1 - my_far)

    def place(y_at, dz):
        low, high = lax.rem(dz, 2), lax.div(dz, 2)
        z_at = my_z + low * (1 - 2 * lax.rem(my_z, 2)) + 2 * high * (1 - 2 * lax.div(my_z, 2))
        return z_at * Y + lax.rem(y_at + Y, Y)

    def target(slot):
        dy, dz = offsets(slot)
        return place(my_y + dy, dz)

    def origin(slot):
        dy, dz = offsets(slot)
        return place(my_y - dy, dz)

    def x_clip(dx, far):
        return lax.rem(my_x + dx, 4) * 2 + far

    barrier = pltpu.get_barrier_semaphore()

    def greet(slot, carry):
        pl.semaphore_signal(barrier, inc=1, device_id={"sp": target(slot)}, device_id_type=MESH)
        return carry

    lax.fori_loop(1, PEERS, greet, 0)
    pl.semaphore_signal(barrier, inc=1, device_id={"cfg": 1 - core}, device_id_type=MESH)
    pl.semaphore_signal(barrier, inc=1, device_id={"clip": far_clip}, device_id_type=MESH)
    for dx in range(1, 4):
        pl.semaphore_signal(
            barrier, inc=1, device_id={"clip": x_clip(dx, my_far)}, device_id_type=MESH
        )

    def slab(ref, at):
        return ref.at[:, pl.ds(pl.multiple_of(at * HEAD_SIZE, HEAD_SIZE), HEAD_SIZE)]

    pairs = ((k_ref, k_buf), (v_ref, v_buf), (c_ref, c_buf), (q_ref, q_buf))
    for at, (ref, buf) in enumerate(pairs):
        pltpu.make_async_copy(slab(ref, sp), buf.at[0], recv_sem.at[at, 0]).start()
    own_text = [
        pltpu.make_async_copy(tk_ref, tk_buf.at[clip], local_sem.at[0]),
        pltpu.make_async_copy(tv_ref, tv_buf.at[clip], local_sem.at[1]),
    ]
    own_weight = pltpu.make_async_copy(slab(w_ref, sp), w_buf, local_sem.at[2])
    for copy in own_text:
        copy.start()
    own_weight.start()

    pl.semaphore_wait(barrier, PEERS - 1 + 1 + 1 + 3)

    def moved(at, slot):
        ref, buf = pairs[at]
        to = target(slot)
        return pltpu.make_async_remote_copy(
            src_ref=slab(ref, to),
            dst_ref=buf.at[slot],
            send_sem=send_sem.at[at, slot],
            recv_sem=recv_sem.at[at, slot],
            device_id={"sp": to},
            device_id_type=MESH,
        )

    texts = ((tk_ref, tk_buf), (tv_ref, tv_buf))

    def text_copy(at, lane):
        ref, buf = texts[at]
        if lane == 0:
            to, source, chunk = far_clip, ref, clip
        elif lane < 4:
            to, source, chunk = x_clip(lane, my_far), ref, clip
        else:
            to, source, chunk = x_clip(lane - 3, my_far), buf.at[far_clip], far_clip
        return pltpu.make_async_remote_copy(
            src_ref=source,
            dst_ref=buf.at[chunk],
            send_sem=text_send.at[at, lane],
            recv_sem=text_recv.at[at, lane],
            device_id={"clip": to},
            device_id_type=MESH,
        )

    for lane in range(4):
        for at in range(2):
            text_copy(at, lane).start()

    def send_one(at):
        def body(slot, carry):
            moved(at, slot).start()
            return carry

        lax.fori_loop(1, PEERS, body, 0)

    send_one(0)
    for at in range(2):
        text_copy(at, 0).wait_recv()
    for lane in range(4, 7):
        for at in range(2):
            text_copy(at, lane).start()
    send_one(1)

    def send_queries(slot, carry):
        moved(2, slot).start()
        moved(3, slot).start()
        return carry

    lax.fori_loop(1, PEERS, send_queries, 0)

    own_weight.wait()
    weight = w_buf[...]
    for half in range(2):
        for group in range(4):
            channel = lax.broadcasted_iota(jnp.int32, (64, 128), 0) - 32 * half
            lane = lax.broadcasted_iota(jnp.int32, (64, 128), 1) - 32 * group
            chosen = (channel == lane) & (lane >= 0) & (lane < 32)
            chosen = jnp.where(chosen, 1.0, 0.0).astype(jnp.bfloat16)
            spread[pl.ds(group * 128, 128), pl.ds(half * 128, 128)] = lax.dot_general(
                weight, chosen, TN, preferred_element_type=jnp.float32
            ).astype(jnp.bfloat16)

    position = jnp.full((1, TOKENS), step_ref[0], jnp.int32).astype(jnp.float32)
    sigma_now = sigma_at(position)
    sigma_next = sigma_at(position + 1.0)
    sigma_prev = sigma_at(position - 1.0)
    lambda_now = log_ratio(sigma_now)
    h_value = log_ratio(sigma_next) - lambda_now
    phi_value = jnp.exp(-h_value) - 1.0
    ratio = (log_ratio(sigma_prev) - lambda_now) / h_value
    text_limit = limit_ref[0]
    coefficient = jnp.where(core == 0, guide_scale, 1.0 - guide_scale)

    for copy in own_text:
        copy.wait()
    for lane in range(1, 7):
        for at in range(2):
            text_copy(at, lane).wait_recv()

    for at in range(2):
        ref, buf = pairs[at]
        pltpu.make_async_copy(slab(ref, sp), buf.at[0], recv_sem.at[at, 0]).wait()

    def arrived(slot, carry):
        moved(0, slot).wait_recv()
        moved(1, slot).wait_recv()
        return carry

    lax.fori_loop(1, PEERS, arrived, 0)

    def to_partner(pair):
        return pltpu.make_async_remote_copy(
            src_ref=part_out.at[pair],
            dst_ref=part_in.at[pair],
            send_sem=part_send.at[pair],
            recv_sem=part_recv.at[pair],
            device_id={"cfg": 1 - core},
            device_id_type=MESH,
        )

    def to_owner(slot):
        return pltpu.make_async_remote_copy(
            src_ref=back_out.at[slot],
            dst_ref=back_in.at[slot],
            send_sem=back_send.at[slot],
            recv_sem=back_recv.at[slot],
            device_id={"sp": origin(slot)},
            device_id_type=MESH,
        )

    def wait_queries(slot):
        for at in (2, 3):
            moved(at, slot).wait_recv()

    def finish(pair):
        to_partner(pair).wait_recv()
        both = mine[pair] + part_in[pair]
        back_out[2 * pair] = both[:PACK]
        back_out[2 * pair + 1] = both[PACK:]

        @pl.when(pair > 0)
        def _():
            to_owner(2 * pair).start()

        to_owner(2 * pair + 1).start()

    def one_pair(pair, carry):
        @pl.when(pair == 0)
        def _():
            for at in (2, 3):
                ref, buf = pairs[at]
                pltpu.make_async_copy(slab(ref, sp), buf.at[0], recv_sem.at[at, 0]).wait()

        @pl.when(pair > 0)
        def _():
            wait_queries(2 * pair)

        wait_queries(2 * pair + 1)
        rows = 2 * TOKENS
        keys = k_buf[...].reshape(PEERS * TOKENS, HEAD_SIZE)
        values = v_buf[...].reshape(PEERS * TOKENS, HEAD_SIZE)
        queries = q_buf[pl.ds(2 * pair, 2)].reshape(rows, HEAD_SIZE)
        crossing = c_buf[pl.ds(2 * pair, 2)].reshape(rows, HEAD_SIZE)
        prompt_keys = tk_buf[...].reshape(512, HEAD_SIZE)
        prompt_values = tv_buf[...].reshape(512, HEAD_SIZE)
        self_out = attend(queries, keys, values, None)
        cross_out = attend(crossing, prompt_keys, prompt_values, text_limit)
        attended = (self_out + cross_out).astype(jnp.bfloat16).astype(jnp.float32)
        packed = []
        for first in (0, TOKENS):
            groups = [attended[first + PACK * g : first + PACK * (g + 1)] for g in range(3)]
            last = attended[first + 3 * PACK : first + TOKENS]
            padding = jnp.zeros((4 * PACK - TOKENS, HEAD_SIZE), jnp.float32)
            groups.append(jnp.concatenate([last, padding], axis=0))
            packed.append(jnp.concatenate(groups, axis=1))
        packed = jnp.concatenate(packed, axis=0).astype(jnp.bfloat16)
        product = coefficient * jnp.dot(packed, spread[...], preferred_element_type=jnp.float32)
        low, high = product[:, :128], product[:, 128:]
        mine[pair] = jnp.where(core == 0, low, high)
        part_out[pair] = jnp.where(core == 0, high, low)
        to_partner(pair).start()

        @pl.when(pair > 0)
        def _():
            finish(pair - 1)

        return carry

    lax.fori_loop(0, PAIRS, one_pair, 0)
    finish(PAIRS - 1)

    def returned(slot, carry):
        to_owner(slot).wait_recv()
        return carry + back_in[slot]

    total = lax.fori_loop(1, PEERS, returned, back_out[0])
    square = jnp.concatenate([total, jnp.zeros((128 - PACK, 128), jnp.float32)], axis=0).T
    token = lax.broadcasted_iota(jnp.int32, (32, 128), 1)
    velocity = square[:32]
    for group in range(1, 4):
        shifted = pltpu.roll(square[32 * group : 32 * (group + 1)], PACK * group, 1)
        velocity = jnp.where(token < PACK * group, velocity, shifted)
    velocity = velocity[:, :TOKENS]
    latent = latent_ref[...]
    denoised = latent - sigma_now * velocity
    difference = (denoised - previous_ref[...]) / ratio
    denoised_ref[...] = denoised
    next_ref[...] = (
        sigma_next / sigma_now * latent
        - (1.0 - sigma_next) * phi_value * denoised
        - 0.5 * (1.0 - sigma_next) * phi_value * difference
    )

    def sent(slot, carry):
        for at in range(4):
            moved(at, slot).wait_send()
        to_owner(slot).wait_send()
        return carry

    lax.fori_loop(1, PEERS, sent, 0)
    for lane in range(7):
        for at in range(2):
            text_copy(at, lane).wait_send()

    def part_sent(pair, carry):
        to_partner(pair).wait_send()
        return carry

    lax.fori_loop(0, PAIRS, part_sent, 0)


def on_device(
    self_queries,
    self_keys,
    self_values,
    cross_queries,
    text_keys,
    text_values,
    text_lengths,
    head_weight,
    latent,
    previous_denoised,
    step_index,
):
    flat = lambda array: array.reshape(array.shape[-2], array.shape[-1])
    vmem = pl.BlockSpec(memory_space=pltpu.VMEM)
    smem = pl.BlockSpec(memory_space=pltpu.SMEM)
    anywhere = pl.BlockSpec(memory_space=pl.ANY)
    block = pltpu.VMEM((PEERS, TOKENS, HEAD_SIZE), jnp.bfloat16)
    prompt = pltpu.VMEM((8, 64, HEAD_SIZE), jnp.bfloat16)
    paired = pltpu.VMEM((PAIRS, 2 * PACK, 128), jnp.float32)
    single = pltpu.VMEM((PEERS, PACK, 128), jnp.float32)
    dma = pltpu.SemaphoreType.DMA
    out = jax.ShapeDtypeStruct((32, TOKENS), jnp.float32)
    denoised, next_latent = pl.pallas_call(
        kernel,
        out_shape=(out, out),
        in_specs=[smem, smem] + [anywhere] * 7 + [vmem] * 2,
        out_specs=(vmem, vmem),
        scratch_shapes=[block] * 4
        + [prompt] * 2
        + [pltpu.VMEM((64, HEAD_SIZE), jnp.bfloat16), pltpu.VMEM((512, 256), jnp.bfloat16)]
        + [paired] * 3
        + [single] * 2
        + [dma((4, PEERS)), dma((4, PEERS)), dma((2, 7)), dma((2, 7)), dma((3,))]
        + [dma((PAIRS,)), dma((PAIRS,)), dma((PEERS,)), dma((PEERS,))],
        compiler_params=pltpu.CompilerParams(
            collective_id=0, has_side_effects=True, vmem_limit_bytes=62 * 2**20
        ),
        name="denoise",
    )(
        text_lengths,
        step_index,
        flat(self_queries),
        flat(self_keys),
        flat(self_values),
        flat(cross_queries),
        flat(text_keys),
        flat(text_values),
        head_weight.T,
        flat(latent).T,
        flat(previous_denoised).T,
    )
    return (denoised.T[None], next_latent.T[None])


def solution(mesh):
    return jax.shard_map(
        on_device,
        mesh=mesh,
        in_specs=(
            P("clip", "cfg", "sp", None),
            P("clip", "cfg", "sp", None),
            P("clip", "cfg", "sp", None),
            P("clip", "cfg", "sp", None),
            P("cfg", "clip", "sp"),
            P("cfg", "clip", "sp"),
            P("cfg"),
            P(),
            P("clip", "sp", "cfg"),
            P("clip", "sp", "cfg"),
            P("clip"),
        ),
        out_specs=(P("clip", "sp", "cfg"), P("clip", "sp", "cfg")),
        check_vma=False,
    )
```

time: 246 us -> 101 us (0.41)
  the two profiles are of different devices: /device:TPU:1 before, /device:TPU:41 now
where the time goes in v1:
time: 101 us
  Pallas kernels  96.7 us (96%)
  local copies, waits for them, and re-layouts  1.94 us (2%)
  between operations  1.94 us (2%)
    pallas_call x1, Pallas kernels, on_device(): pl.pallas_call(kernel, out_shape=(out, out), in_specs=[smem, smem] + [any...  96.7 us

profile of v1, /device:TPU:41, one launch (start us, length us, event | category | flops | bytes accessed | tf_op | source)
XLA Modules:
  0.0 100.5 jit_solution(9740483863597234146)
XLA Ops:
  1.9 96.7 %denoise.1 = (f32[32,80]{1,0:T(8,128)}, f32[32,80]{1,0:T(8,128)}) custom-call(s32[1]{0:T(128)S(6)} %copy.15.limit_ref, s32[1]{0:T(128)S(6)} %copy.16.step_ref, bf16[80,4096]{1,0:T(8,128)(2,1)} %bitcast.19, bf16[80,4096]{1,0:T(8,128)(2,1)} %bitcast.20, bf16[80,4096]{1,0:T(8,128)(2,1)} %bitcast.21, bf16[80,4096]{1,0:T(8,128)(2,1)} %bitcast.22, ...), custom_call_target="tpu_custom_call" | custom-call | tf_op jit(solution)/shard_map/denoise/pallas_call | solution.py:388
  98.6 0.0 copy-start
  98.6 1.3 %copy.17 = f32[1,80,32]{1,2,0:T(8,128)} copy(f32[1,80,32]{1,2,0:T(8,128)} %bitcast.29) | data formatting | bytes 20480
  99.9 0.0 copy-done
  99.9 0.6 copy.18
Async XLA Ops:
  98.6 1.3 %copy-start = (f32[32,80]{1,0:T(8,128)S(1)}, f32[32,80]{1,0:T(8,128)}, u32[]{:S(2)}) copy-start(f32[32,80]{1,0:T(8,128)} %get-tuple-element.5) | copy-start | bytes 30724

commit v2 on v1

--- a/solution.py
+++ b/solution.py
@@ -63,10 +63,7 @@
     tk_ref,
     tv_ref,
     w_ref,
-    latent_ref,
-    previous_ref,
-    denoised_ref,
-    next_ref,
+    out_ref,
     q_buf,
     k_buf,
     v_buf,
@@ -81,7 +78,8 @@
     back_out,
     back_in,
     send_sem,
-    recv_sem,
+    whole_recv,
+    pair_recv,
     text_send,
     text_recv,
     local_sem,
@@ -121,7 +119,11 @@
 
     lax.fori_loop(1, PEERS, greet, 0)
     pl.semaphore_signal(barrier, inc=1, device_id={"cfg": 1 - core}, device_id_type=MESH)
-    pl.semaphore_signal(barrier, inc=1, device_id={"clip": far_clip}, device_id_type=MESH)
+
+    @pl.when(my_far == 0)
+    def _():
+        pl.semaphore_signal(barrier, inc=1, device_id={"clip": far_clip}, device_id_type=MESH)
+
     for dx in range(1, 4):
         pl.semaphore_signal(
             barrier, inc=1, device_id={"clip": x_clip(dx, my_far)}, device_id_type=MESH
@@ -130,19 +132,21 @@
     def slab(ref, at):
         return ref.at[:, pl.ds(pl.multiple_of(at * HEAD_SIZE, HEAD_SIZE), HEAD_SIZE)]
 
+    def arrival(at, slot):
+        return whole_recv.at[at] if at < 2 else pair_recv.at[at - 2, lax.div(slot, 2)]
+
+    def await_bytes(part, sem):
+        pltpu.make_async_copy(part, part, sem).wait()
+
     pairs = ((k_ref, k_buf), (v_ref, v_buf), (c_ref, c_buf), (q_ref, q_buf))
     for at, (ref, buf) in enumerate(pairs):
-        pltpu.make_async_copy(slab(ref, sp), buf.at[0], recv_sem.at[at, 0]).start()
-    own_text = [
-        pltpu.make_async_copy(tk_ref, tk_buf.at[clip], local_sem.at[0]),
-        pltpu.make_async_copy(tv_ref, tv_buf.at[clip], local_sem.at[1]),
-    ]
-    own_weight = pltpu.make_async_copy(slab(w_ref, sp), w_buf, local_sem.at[2])
-    for copy in own_text:
-        copy.start()
+        pltpu.make_async_copy(slab(ref, sp), buf.at[0], arrival(at, 0)).start()
+    pltpu.make_async_copy(tk_ref, tk_buf.at[clip], text_recv.at[0, 1]).start()
+    pltpu.make_async_copy(tv_ref, tv_buf.at[clip], text_recv.at[1, 1]).start()
+    own_weight = pltpu.make_async_copy(slab(w_ref, sp), w_buf, local_sem.at[0])
     own_weight.start()
 
-    pl.semaphore_wait(barrier, PEERS - 1 + 1 + 1 + 3)
+    pl.semaphore_wait(barrier, PEERS - 1 + 1 + 3 + my_far)
 
     def moved(at, slot):
         ref, buf = pairs[at]
@@ -150,8 +154,8 @@
         return pltpu.make_async_remote_copy(
             src_ref=slab(ref, to),
             dst_ref=buf.at[slot],
-            send_sem=send_sem.at[at, slot],
-            recv_sem=recv_sem.at[at, slot],
+            send_sem=send_sem.at[at],
+            recv_sem=arrival(at, slot),
             device_id={"sp": to},
             device_id_type=MESH,
         )
@@ -169,13 +173,18 @@
         return pltpu.make_async_remote_copy(
             src_ref=source,
             dst_ref=buf.at[chunk],
-            send_sem=text_send.at[at, lane],
-            recv_sem=text_recv.at[at, lane],
+            send_sem=text_send.at[at],
+            recv_sem=text_recv.at[at, min(lane, 1)],
             device_id={"clip": to},
             device_id_type=MESH,
         )
 
-    for lane in range(4):
+    @pl.when(my_far == 1)
+    def _():
+        for at in range(2):
+            text_copy(at, 0).start()
+
+    for lane in range(1, 4):
         for at in range(2):
             text_copy(at, lane).start()
 
@@ -189,6 +198,12 @@
     send_one(0)
     for at in range(2):
         text_copy(at, 0).wait_recv()
+
+    @pl.when(my_far == 0)
+    def _():
+        for at in range(2):
+            text_copy(at, 0).start()
+
     for lane in range(4, 7):
         for at in range(2):
             text_copy(at, lane).start()
@@ -213,39 +228,29 @@
                 weight, chosen, TN, preferred_element_type=jnp.float32
             ).astype(jnp.bfloat16)
 
-    position = jnp.full((1, TOKENS), step_ref[0], jnp.int32).astype(jnp.float32)
+    position = jnp.broadcast_to(step_ref[...], (1, TOKENS)).astype(jnp.float32)
     sigma_now = sigma_at(position)
     sigma_next = sigma_at(position + 1.0)
-    sigma_prev = sigma_at(position - 1.0)
     lambda_now = log_ratio(sigma_now)
     h_value = log_ratio(sigma_next) - lambda_now
-    phi_value = jnp.exp(-h_value) - 1.0
-    ratio = (log_ratio(sigma_prev) - lambda_now) / h_value
-    text_limit = limit_ref[0]
+    ratio = (log_ratio(sigma_at(position - 1.0)) - lambda_now) / h_value
+    pull = (1.0 - sigma_next) * (jnp.exp(-h_value) - 1.0)
+    for at, value in enumerate((sigma_now, sigma_next / sigma_now, pull, 0.5 * pull / ratio)):
+        out_ref[32 + at : 33 + at] = value
+    out_ref[36:] = jnp.zeros((4, TOKENS), jnp.float32)
+    text_limit = limit_ref[...]
     coefficient = jnp.where(core == 0, guide_scale, 1.0 - guide_scale)
 
-    for copy in own_text:
-        copy.wait()
-    for lane in range(1, 7):
-        for at in range(2):
-            text_copy(at, lane).wait_recv()
-
-    for at in range(2):
-        ref, buf = pairs[at]
-        pltpu.make_async_copy(slab(ref, sp), buf.at[0], recv_sem.at[at, 0]).wait()
-
-    def arrived(slot, carry):
-        moved(0, slot).wait_recv()
-        moved(1, slot).wait_recv()
-        return carry
-
-    lax.fori_loop(1, PEERS, arrived, 0)
+    for at, buf in enumerate((tk_buf, tv_buf)):
+        await_bytes(buf.at[pl.ds(0, 7)], text_recv.at[at, 1])
+    for at, buf in enumerate((k_buf, v_buf)):
+        await_bytes(buf, whole_recv.at[at])
 
     def to_partner(pair):
         return pltpu.make_async_remote_copy(
             src_ref=part_out.at[pair],
             dst_ref=part_in.at[pair],
-            send_sem=part_send.at[pair],
+            send_sem=part_send.at[0],
             recv_sem=part_recv.at[pair],
             device_id={"cfg": 1 - core},
             device_id_type=MESH,
@@ -255,15 +260,11 @@
         return pltpu.make_async_remote_copy(
             src_ref=back_out.at[slot],
             dst_ref=back_in.at[slot],
-            send_sem=back_send.at[slot],
-            recv_sem=back_recv.at[slot],
+            send_sem=back_send.at[0],
+            recv_sem=back_recv.at[0],
             device_id={"sp": origin(slot)},
             device_id_type=MESH,
         )
-
-    def wait_queries(slot):
-        for at in (2, 3):
-            moved(at, slot).wait_recv()
 
     def finish(pair):
         to_partner(pair).wait_recv()
@@ -278,17 +279,8 @@
         to_owner(2 * pair + 1).start()
 
     def one_pair(pair, carry):
-        @pl.when(pair == 0)
-        def _():
-            for at in (2, 3):
-                ref, buf = pairs[at]
-                pltpu.make_async_copy(slab(ref, sp), buf.at[0], recv_sem.at[at, 0]).wait()
-
-        @pl.when(pair > 0)
-        def _():
-            wait_queries(2 * pair)
-
-        wait_queries(2 * pair + 1)
+        for at, buf in enumerate((c_buf, q_buf)):
+            await_bytes(buf.at[pl.ds(2 * pair, 2)], pair_recv.at[at, pair])
         rows = 2 * TOKENS
         keys = k_buf[...].reshape(PEERS * TOKENS, HEAD_SIZE)
         values = v_buf[...].reshape(PEERS * TOKENS, HEAD_SIZE)
@@ -322,44 +314,22 @@
     lax.fori_loop(0, PAIRS, one_pair, 0)
     finish(PAIRS - 1)
 
-    def returned(slot, carry):
-        to_owner(slot).wait_recv()
-        return carry + back_in[slot]
-
-    total = lax.fori_loop(1, PEERS, returned, back_out[0])
+    await_bytes(back_in.at[pl.ds(1, PEERS - 1)], back_recv.at[0])
+    total = back_out[0] + jnp.sum(back_in[pl.ds(1, PEERS - 1)], axis=0)
     square = jnp.concatenate([total, jnp.zeros((128 - PACK, 128), jnp.float32)], axis=0).T
     token = lax.broadcasted_iota(jnp.int32, (32, 128), 1)
     velocity = square[:32]
     for group in range(1, 4):
         shifted = pltpu.roll(square[32 * group : 32 * (group + 1)], PACK * group, 1)
         velocity = jnp.where(token < PACK * group, velocity, shifted)
-    velocity = velocity[:, :TOKENS]
-    latent = latent_ref[...]
-    denoised = latent - sigma_now * velocity
-    difference = (denoised - previous_ref[...]) / ratio
-    denoised_ref[...] = denoised
-    next_ref[...] = (
-        sigma_next / sigma_now * latent
-        - (1.0 - sigma_next) * phi_value * denoised
-        - 0.5 * (1.0 - sigma_next) * phi_value * difference
-    )
-
-    def sent(slot, carry):
-        for at in range(4):
-            moved(at, slot).wait_send()
-        to_owner(slot).wait_send()
-        return carry
-
-    lax.fori_loop(1, PEERS, sent, 0)
-    for lane in range(7):
-        for at in range(2):
-            text_copy(at, lane).wait_send()
-
-    def part_sent(pair, carry):
-        to_partner(pair).wait_send()
-        return carry
-
-    lax.fori_loop(0, PAIRS, part_sent, 0)
+    out_ref[:32] = velocity[:, :TOKENS]
+
+    for at, (ref, buf) in enumerate(pairs):
+        await_bytes(buf.at[pl.ds(1, PEERS - 1)], send_sem.at[at])
+    for at, buf in enumerate((tk_buf, tv_buf)):
+        await_bytes(buf.at[pl.ds(0, 7)], text_send.at[at])
+    await_bytes(back_out.at[pl.ds(1, PEERS - 1)], back_send.at[0])
+    await_bytes(part_out, part_send.at[0])
 
 
 def on_device(
@@ -377,33 +347,31 @@
 ):
     flat = lambda array: array.reshape(array.shape[-2], array.shape[-1])
     vmem = pl.BlockSpec(memory_space=pltpu.VMEM)
-    smem = pl.BlockSpec(memory_space=pltpu.SMEM)
     anywhere = pl.BlockSpec(memory_space=pl.ANY)
     block = pltpu.VMEM((PEERS, TOKENS, HEAD_SIZE), jnp.bfloat16)
     prompt = pltpu.VMEM((8, 64, HEAD_SIZE), jnp.bfloat16)
     paired = pltpu.VMEM((PAIRS, 2 * PACK, 128), jnp.float32)
     single = pltpu.VMEM((PEERS, PACK, 128), jnp.float32)
     dma = pltpu.SemaphoreType.DMA
-    out = jax.ShapeDtypeStruct((32, TOKENS), jnp.float32)
-    denoised, next_latent = pl.pallas_call(
+    result = pl.pallas_call(
         kernel,
-        out_shape=(out, out),
-        in_specs=[smem, smem] + [anywhere] * 7 + [vmem] * 2,
-        out_specs=(vmem, vmem),
+        out_shape=jax.ShapeDtypeStruct((40, TOKENS), jnp.float32),
+        in_specs=[vmem] * 2 + [anywhere] * 7,
+        out_specs=vmem,
         scratch_shapes=[block] * 4
         + [prompt] * 2
         + [pltpu.VMEM((64, HEAD_SIZE), jnp.bfloat16), pltpu.VMEM((512, 256), jnp.bfloat16)]
         + [paired] * 3
         + [single] * 2
-        + [dma((4, PEERS)), dma((4, PEERS)), dma((2, 7)), dma((2, 7)), dma((3,))]
-        + [dma((PAIRS,)), dma((PAIRS,)), dma((PEERS,)), dma((PEERS,))],
+        + [dma((4,)), dma((2,)), dma((2, PAIRS)), dma((2,)), dma((2, 2)), dma((1,))]
+        + [dma((1,)), dma((PAIRS,)), dma((1,)), dma((1,))],
         compiler_params=pltpu.CompilerParams(
             collective_id=0, has_side_effects=True, vmem_limit_bytes=62 * 2**20
         ),
         name="denoise",
     )(
-        text_lengths,
-        step_index,
+        text_lengths.reshape(1, 1),
+        step_index.reshape(1, 1),
         flat(self_queries),
         flat(self_keys),
         flat(self_values),
@@ -411,10 +379,12 @@
         flat(text_keys),
         flat(text_values),
         head_weight.T,
-        flat(latent).T,
-        flat(previous_denoised).T,
     )
-    return (denoised.T[None], next_latent.T[None])
+    velocity = result[:32].T[None]
+    sigma_now, keep, pull, push = (result[32 + at][None, :, None] for at in range(4))
+    denoised = latent - sigma_now * velocity
+    next_latent = keep * latent - pull * denoised - push * (denoised - previous_denoised)
+    return (denoised, next_latent)
 
 
 def solution(mesh):

time: 101 us -> 92.9 us (0.920)
  the two profiles are of different devices: /device:TPU:41 before, /device:TPU:1 now
where the time goes in v2:
time: 92.9 us; the launch traced here: 92.4 us
  Pallas kernels  88.3 us (95%)
  between operations  1.95 us (2%)
  other arithmetic  1.34 us (1%)
    pallas_call x1, Pallas kernels, on_device(): pl.pallas_call(kernel, out_shape=jax.ShapeDtypeStruct((40, TOKENS), jnp.f...  88.3 us

profile of v2, /device:TPU:1, one launch (start us, length us, event | category | flops | bytes accessed | tf_op | source)
XLA Modules:
  0.0 92.4 jit_solution(2481360605610338132)
XLA Ops:
  1.9 0.0 copy-start
  1.9 0.0 copy-start.1
  1.9 88.3 %denoise.1 = f32[40,80]{1,0:T(8,128)} custom-call(s32[1,1]{1,0:T(1,128)} %bitcast.22.limit_ref, s32[1,1]{1,0:T(1,128)} %bitcast.23.step_ref, bf16[80,4096]{1,0:T(8,128)(2,1)} %bitcast.24, bf16[80,4096]{1,0:T(8,128)(2,1)} %bitcast.25, bf16[80,4096]{1,0:T(8,128)(2,1)} %bitcast.26, bf16[80,4096]{1,0:T(8,128)(2,1)} %bitcast.27, bf16[64,128]{1,0:T(8,128)(2,1)} %bitcast.29, ...), custom_call_target="tpu_custom_call" | custom-call | tf_op jit(solution)/shard_map/denoise/pallas_call | solution.py:356
  90.2 0.8 slice_bitcast_fusion.3
  91.1 0.0 copy-done
  91.1 0.0 copy-done.1
  91.1 1.3 %multiply_subtract_fusion = (f32[1,80,32]{1,2,0:T(8,128)}, f32[1,80,32]{1,2,0:T(8,128)}) fusion(f32[1,80,32]{1,2,0:T(8,128)S(1)} %copy-done, f32[1,80,32]{1,2,0:T(8,128)S(1)} %copy-done.1, f32[80]{0:T(128)S(1)} %get-tuple-element.5, f32[80]{0:T(128)S(1)} %get-tuple-element.6, f32[80]{0:T(128)S(1)} %get-tuple-element.7, f32[40,80]{1,0:T(8,128)} %denoise.1, ...), kind=kLoop, calls=%fused_computation.1 | loop fusion | flops 20480 | bytes 52480 | tf_op jit(solution)/shard_map/sub | solution.py:386
Async XLA Ops:
  1.9 89.2 %copy-start = (f32[1,80,32]{1,2,0:T(8,128)S(1)}, f32[1,80,32]{1,2,0:T(8,128)}, u32[]{:S(2)}) copy-start(f32[1,80,32]{1,2,0:T(8,128)} %param.20) | copy-start | bytes 30724
  1.9 89.1 %copy-start.1 = (f32[1,80,32]{1,2,0:T(8,128)S(1)}, f32[1,80,32]{1,2,0:T(8,128)}, u32[]{:S(2)}) copy-start(f32[1,80,32]{1,2,0:T(8,128)} %param.19) | copy-start | bytes 30724

commit v3 on v2

--- a/solution.py
+++ b/solution.py
@@ -63,6 +63,8 @@
     tk_ref,
     tv_ref,
     w_ref,
+    latent_ref,
+    previous_ref,
     out_ref,
     q_buf,
     k_buf,
@@ -71,6 +73,8 @@
     tk_buf,
     tv_buf,
     w_buf,
+    latent_buf,
+    previous_buf,
     spread,
     mine,
     part_out,
@@ -144,7 +148,10 @@
     pltpu.make_async_copy(tk_ref, tk_buf.at[clip], text_recv.at[0, 1]).start()
     pltpu.make_async_copy(tv_ref, tv_buf.at[clip], text_recv.at[1, 1]).start()
     own_weight = pltpu.make_async_copy(slab(w_ref, sp), w_buf, local_sem.at[0])
-    own_weight.start()
+    own_latent = pltpu.make_async_copy(latent_ref, latent_buf, local_sem.at[1])
+    own_previous = pltpu.make_async_copy(previous_ref, previous_buf, local_sem.at[2])
+    for copy in (own_weight, own_latent, own_previous):
+        copy.start()
 
     pl.semaphore_wait(barrier, PEERS - 1 + 1 + 3 + my_far)
 
@@ -235,9 +242,7 @@
     h_value = log_ratio(sigma_next) - lambda_now
     ratio = (log_ratio(sigma_at(position - 1.0)) - lambda_now) / h_value
     pull = (1.0 - sigma_next) * (jnp.exp(-h_value) - 1.0)
-    for at, value in enumerate((sigma_now, sigma_next / sigma_now, pull, 0.5 * pull / ratio)):
-        out_ref[32 + at : 33 + at] = value
-    out_ref[36:] = jnp.zeros((4, TOKENS), jnp.float32)
+    keep, push = sigma_next / sigma_now, 0.5 * pull / ratio
     text_limit = limit_ref[...]
     coefficient = jnp.where(core == 0, guide_scale, 1.0 - guide_scale)
 
@@ -322,7 +327,12 @@
     for group in range(1, 4):
         shifted = pltpu.roll(square[32 * group : 32 * (group + 1)], PACK * group, 1)
         velocity = jnp.where(token < PACK * group, velocity, shifted)
-    out_ref[:32] = velocity[:, :TOKENS]
+    own_latent.wait()
+    own_previous.wait()
+    latent = latent_buf[...]
+    denoised = latent - sigma_now * velocity[:, :TOKENS]
+    out_ref[:32] = denoised
+    out_ref[32:] = keep * latent - pull * denoised - push * (denoised - previous_buf[...])
 
     for at, (ref, buf) in enumerate(pairs):
         await_bytes(buf.at[pl.ds(1, PEERS - 1)], send_sem.at[at])
@@ -355,15 +365,17 @@
     dma = pltpu.SemaphoreType.DMA
     result = pl.pallas_call(
         kernel,
-        out_shape=jax.ShapeDtypeStruct((40, TOKENS), jnp.float32),
-        in_specs=[vmem] * 2 + [anywhere] * 7,
+        out_shape=jax.ShapeDtypeStruct((64, TOKENS), jnp.float32),
+        in_specs=[vmem] * 2 + [anywhere] * 9,
         out_specs=vmem,
         scratch_shapes=[block] * 4
         + [prompt] * 2
-        + [pltpu.VMEM((64, HEAD_SIZE), jnp.bfloat16), pltpu.VMEM((512, 256), jnp.bfloat16)]
+        + [pltpu.VMEM((64, HEAD_SIZE), jnp.bfloat16)]
+        + [pltpu.VMEM((32, TOKENS), jnp.float32)] * 2
+        + [pltpu.VMEM((512, 256), jnp.bfloat16)]
         + [paired] * 3
         + [single] * 2
-        + [dma((4,)), dma((2,)), dma((2, PAIRS)), dma((2,)), dma((2, 2)), dma((1,))]
+        + [dma((4,)), dma((2,)), dma((2, PAIRS)), dma((2,)), dma((2, 2)), dma((3,))]
         + [dma((1,)), dma((PAIRS,)), dma((1,)), dma((1,))],
         compiler_params=pltpu.CompilerParams(
             collective_id=0, has_side_effects=True, vmem_limit_bytes=62 * 2**20
@@ -379,12 +391,10 @@
         flat(text_keys),
         flat(text_values),
         head_weight.T,
+        flat(latent).T,
+        flat(previous_denoised).T,
     )
-    velocity = result[:32].T[None]
-    sigma_now, keep, pull, push = (result[32 + at][None, :, None] for at in range(4))
-    denoised = latent - sigma_now * velocity
-    next_latent = keep * latent - pull * denoised - push * (denoised - previous_denoised)
-    return (denoised, next_latent)
+    return (result[:32].T[None], result[32:].T[None])
 
 
 def solution(mesh):

time: 92.9 us -> 91.9 us (0.989)
  other arithmetic: 1.34 us -> 0 us
    broadcast_in_dim x0 -> x1, local copies, waits for them, and re-layouts: none -> 1.35 us  [on_device(): return (result[:32].T[None], result[32:].T[None])]
    sub x1 -> x0, other arithmetic: 1.34 us -> none  [on_device(): keep * latent - pull * denoised - push * (denoised - previous_denoised)]
where the time goes in v3:
time: 91.9 us; the launch traced here: 91.4 us
  Pallas kernels  88.2 us (96%)
  between operations  1.93 us (2%)
  local copies, waits for them, and re-layouts  1.35 us (1%)
    pallas_call x1, Pallas kernels, on_device(): pl.pallas_call(kernel, out_shape=jax.ShapeDtypeStruct((64, TOKENS), jnp.f...  88.2 us

profile of v3, /device:TPU:1, one launch (start us, length us, event | category | flops | bytes accessed | tf_op | source)
XLA Modules:
  0.0 91.4 jit_solution(5437209496910930710)
XLA Ops:
  1.9 88.2 %denoise.1 = f32[64,80]{1,0:T(8,128)} custom-call(s32[1,1]{1,0:T(1,128)} %bitcast.23.limit_ref, s32[1,1]{1,0:T(1,128)} %bitcast.24.step_ref, bf16[80,4096]{1,0:T(8,128)(2,1)} %bitcast.25, bf16[80,4096]{1,0:T(8,128)(2,1)} %bitcast.26, bf16[80,4096]{1,0:T(8,128)(2,1)} %bitcast.27, bf16[80,4096]{1,0:T(8,128)(2,1)} %bitcast.28, bf16[64,128]{1,0:T(8,128)(2,1)} %bitcast.30, ...), custom_call_target="tpu_custom_call" | custom-call | tf_op jit(solution)/shard_map/denoise/pallas_call | solution.py:366
  90.1 1.3 %slice_bitcast_fusion = (f32[1,80,32]{1,2,0:T(8,128)}, f32[1,80,32]{1,2,0:T(8,128)}) fusion(f32[64,80]{1,0:T(8,128)} %denoise.1), kind=kLoop, calls=%fused_computation | loop fusion | bytes 40960 | tf_op jit(solution)/shard_map/broadcast_in_dim | solution.py:397
